TPU v7x, 32 devices: a whole 2x2x4 slice. The times are simulated.
32 devices in a mesh: seq: 4 (over z), chan: 8 (over y, x, core).
Axes of the slice: x: 2, y: 2, z: 4, core: 2. Of those that a mesh axis runs over, the one named last changes fastest.
Arguments:
- query_proj: bfloat16 [1024, 1024], P('seq', 'chan'), may hold values from -6 to 6
- key_proj: bfloat16 [1024, 1024], P('seq', 'chan'), may hold values from -6 to 6
- value_proj: bfloat16 [1024, 1024], P('seq', 'chan'), may hold values from -6 to 6
- filter_in: float32 [32, 64], replicated, may hold values from -16 to 16
- filter_bias: float32 [64], replicated, may hold values from -3.140625 to 3.140625
- filter_out: float32 [64, 1024], P(None, 'chan'), may hold values from -0.75 to 0.75
- decay_level: float32 [1024], P('chan'), may hold values from 0 to 1
- skip_gain: float32 [1024], P('chan'), may hold values from -4 to 4
- out_weight: bfloat16 [4096, 1024], P(None, 'chan'), may hold values from -0.25 to 0.25
Outputs:
- mixed: bfloat16 [1024, 4096], P('seq', 'chan')
All inputs are finite; a program needn't handle non-finite values.
Results may differ from a plain program's by a relative error of at most 0.019.
Values may be sent and summed in bfloat16 or wider, within the bound.
A program may use at most 64 MiB of HBM per device.

v0:
```python
import functools
import math

import jax
import jax.numpy as jnp
import numpy as np
from jax import lax
from jax.experimental import pallas as pl
from jax.experimental.pallas import tpu as pltpu
from jax.sharding import PartitionSpec as P

MESH = pl.DeviceIdType.MESH
highest = lax.Precision.HIGHEST


def flipped(index, mask):
    bit, result = 1, index
    while bit <= mask:
        if mask & bit:
            result = result + bit - 2 * bit * ((index // bit) % 2)
        bit *= 2
    return result


def dft_tables(rows):
    freq = np.arange(rows)[:, None]
    size = 2 * rows

    def packed(times):
        angles = (freq * times[None, :] % size) * (2.0 * math.pi / size)
        sines = np.sin(angles)
        sines[0] = 1.0 - 2.0 * (times % 2)
        return np.concatenate([np.cos(angles), sines], axis=0)

    forward = packed(np.arange(rows))
    weight = np.full((2 * rows, 1), 2.0 / size)
    weight[0] = weight[rows] = 1.0 / size
    inverse = (packed(np.arange(rows, size)) * weight * size).T
    return forward, inverse


def feature_table(half_count, seq_count, rows):
    length = seq_count * rows
    freq = np.arange(1, half_count + 1)
    phases = (np.arange(length)[:, None] * freq[None, :] % length) * (2.0 * math.pi / length)
    table = np.concatenate([np.sin(phases), np.cos(phases)], axis=1)
    return table.reshape(seq_count, rows, 2 * half_count)


def sin_turns(turns):
    angle = (turns - jnp.round(turns)) * (2.0 * math.pi)
    square = angle * angle
    total = jnp.full_like(angle, 1.0 / math.factorial(17))
    for order in (15, 13, 11, 9, 7, 5, 3, 1):
        sign = -1.0 if order % 4 == 3 else 1.0
        total = total * square + sign / math.factorial(order)
    return total * angle


def kernel(
    n_seq,
    n_chan,
    q_ref,
    k_ref,
    v_ref,
    fin_ref,
    bias_ref,
    fout_ref,
    level_ref,
    skip_ref,
    feat_ref,
    fwd_ref,
    inv_ref,
    w_ref,
    out_ref,
    x_buf,
    g_buf,
    w_buf,
    spec,
    acc,
    x_send,
    x_recv,
    g_send,
    g_recv,
    w_send,
    w_recv,
    own_sem,
):
    rows, cols = q_ref.shape
    length = rows * n_seq
    width = w_buf.shape[1]
    me_seq = lax.axis_index("seq")
    me_chan = lax.axis_index("chan")

    barrier = pltpu.get_barrier_semaphore()
    for step in range(1, n_seq):
        pl.semaphore_signal(
            barrier, inc=1, device_id={"seq": lax.rem(me_seq + step, n_seq)}, device_id_type=MESH
        )
    for mask in range(1, n_chan):
        pl.semaphore_signal(
            barrier, inc=1, device_id={"chan": flipped(me_chan, mask)}, device_id_type=MESH
        )

    own_weight = pltpu.make_async_copy(
        w_ref.at[pl.ds(pl.multiple_of(me_chan * width, width), width)], w_buf.at[0], own_sem
    )
    own_weight.start()
    mixed_in = k_ref[...].astype(jnp.float32) * v_ref[...].astype(jnp.float32)
    x_buf[0] = mixed_in.astype(jnp.bfloat16)

    def x_copy(step):
        return pltpu.make_async_remote_copy(
            src_ref=x_buf.at[0],
            dst_ref=x_buf.at[step],
            send_sem=x_send.at[step],
            recv_sem=x_recv.at[step],
            device_id={"seq": lax.rem(me_seq + step, n_seq)},
            device_id_type=MESH,
        )

    def w_copy(mask):
        peer = flipped(me_chan, mask)
        return pltpu.make_async_remote_copy(
            src_ref=w_ref.at[pl.ds(pl.multiple_of(peer * width, width), width)],
            dst_ref=w_buf.at[mask],
            send_sem=w_send.at[mask],
            recv_sem=w_recv.at[mask],
            device_id={"chan": peer},
            device_id_type=MESH,
        )

    def g_copy(mask):
        return pltpu.make_async_remote_copy(
            src_ref=g_buf.at[0],
            dst_ref=g_buf.at[mask],
            send_sem=g_send.at[mask],
            recv_sem=g_recv.at[mask],
            device_id={"chan": flipped(me_chan, mask)},
            device_id_type=MESH,
        )

    pl.semaphore_wait(barrier, n_seq + n_chan - 2)
    for step in range(1, n_seq):
        pl.when(me_seq + step < n_seq)(lambda step=step: x_copy(step).start())
    for mask in reversed(range(1, n_chan)):
        w_copy(mask).start()

    levels = jnp.maximum(2.0 * level_ref[...] - 1.0, 0.0)
    rate = 0.5 / length * jnp.exp(levels * math.log(length / 16.0))
    fin = fin_ref[...] * (0.5 / math.pi)
    bias = bias_ref[...] * (0.5 / math.pi)
    fout = fout_ref[...]

    def tap_block(block, squares):
        turns = jnp.dot(
            feat_ref[block], fin, precision=highest, preferred_element_type=jnp.float32
        )
        hidden = sin_turns(turns + bias)
        raw = jnp.dot(hidden, fout, precision=highest, preferred_element_type=jnp.float32)
        place = lax.broadcasted_iota(jnp.int32, (rows, cols), 0) + block * rows
        taps = raw * jnp.exp(-rate * place.astype(jnp.float32))
        spec[block + 1] = jnp.dot(
            fwd_ref[...], taps.astype(jnp.bfloat16), preferred_element_type=jnp.float32
        )
        return squares + jnp.sum(taps * taps, axis=0, keepdims=True)

    spec[0] = jnp.zeros_like(spec[0])
    squares = jnp.zeros((1, cols), jnp.float32)
    if n_seq <= 4:
        for block in range(n_seq):
            squares = tap_block(block, squares)
    else:
        squares = lax.fori_loop(0, n_seq, tap_block, squares)
    scale = lax.rsqrt(squares + 1e-05)

    row_index = lax.broadcasted_iota(jnp.int32, (rows, cols), 0)
    alternate = (1 - 2 * (row_index % 2)).astype(jnp.float32)

    def add_block(step):
        if step > 0:
            x_copy(step).wait_recv()
        field = jnp.dot(fwd_ref[...], x_buf[step], preferred_element_type=jnp.float32)
        x_cos, x_sin = field[:rows], field[rows:]
        h_cos = spec[step, :rows] + alternate * spec[step + 1, :rows]
        h_sin = spec[step, rows:] + alternate * spec[step + 1, rows:]
        terms = (x_cos * h_cos, x_sin * h_sin, x_cos * h_sin + x_sin * h_cos)
        for place, term in enumerate(terms):
            acc[place] = term if step == 0 else acc[place] + term

    for step in range(n_seq):
        if step == 0:
            add_block(step)
        else:
            pl.when(me_seq >= step)(lambda step=step: add_block(step))

    edge = row_index == 0
    y_cos = acc[0] - jnp.where(edge, 0.0, acc[1])
    y_sin = jnp.where(edge, acc[1], acc[2])
    field = jnp.concatenate([y_cos, y_sin], axis=0) * (0.5 / rows)
    convolved = jnp.dot(
        inv_ref[...], field.astype(jnp.bfloat16), preferred_element_type=jnp.float32
    )
    mixed_in = k_ref[...].astype(jnp.float32) * v_ref[...].astype(jnp.float32)
    gated = q_ref[...].astype(jnp.float32) * (convolved * scale + skip_ref[...] * mixed_in)
    g_buf[0] = gated.astype(jnp.bfloat16)
    for mask in reversed(range(1, n_chan)):
        g_copy(mask).start()

    own_weight.wait()
    total = None
    for pair in range(0, n_chan, 2):
        for mask in (pair, pair + 1):
            if mask > 0:
                w_copy(mask).wait_recv()
                g_copy(mask).wait_recv()
        left = jnp.concatenate([g_buf[pair], g_buf[pair + 1]], axis=1)
        right = jnp.concatenate([w_buf[pair], w_buf[pair + 1]], axis=1)
        part = lax.dot_general(
            left, right, (((1,), (1,)), ((), ())), preferred_element_type=jnp.float32
        )
        total = part if total is None else total + part
    out_ref[...] = total.astype(out_ref.dtype)

    for step in range(1, n_seq):
        pl.when(me_seq + step < n_seq)(lambda step=step: x_copy(step).wait_send())
    for mask in range(1, n_chan):
        w_copy(mask).wait_send()
        g_copy(mask).wait_send()


def solution(mesh):
    n_seq, n_chan = mesh.shape["seq"], mesh.shape["chan"]

    def body(query, key, value, fin, bias, fout, level, skip, weight):
        rows, cols = query.shape
        width = weight.shape[0] // n_chan
        forward, inverse = dft_tables(rows)
        features = feature_table(fin.shape[0] // 2, n_seq, rows)
        vmem = pl.BlockSpec(memory_space=pltpu.VMEM)
        return pl.pallas_call(
            functools.partial(kernel, n_seq, n_chan),
            out_shape=jax.ShapeDtypeStruct((rows, width), jnp.bfloat16),
            in_specs=[vmem] * 11 + [pl.BlockSpec(memory_space=pl.ANY)],
            out_specs=vmem,
            scratch_shapes=[
                pltpu.VMEM((n_seq, rows, cols), jnp.bfloat16),
                pltpu.VMEM((n_chan, rows, cols), jnp.bfloat16),
                pltpu.VMEM((n_chan, width, cols), jnp.bfloat16),
                pltpu.VMEM((n_seq + 1, 2 * rows, cols), jnp.float32),
                pltpu.VMEM((3, rows, cols), jnp.float32),
                pltpu.SemaphoreType.DMA((n_seq,)),
                pltpu.SemaphoreType.DMA((n_seq,)),
                pltpu.SemaphoreType.DMA((n_chan,)),
                pltpu.SemaphoreType.DMA((n_chan,)),
                pltpu.SemaphoreType.DMA((n_chan,)),
                pltpu.SemaphoreType.DMA((n_chan,)),
                pltpu.SemaphoreType.DMA,
            ],
            compiler_params=pltpu.CompilerParams(
                collective_id=0, has_side_effects=True, vmem_limit_bytes=40 * 1024 * 1024
            ),
        )(
            query,
            key,
            value,
            fin,
            bias.reshape(1, -1),
            fout,
            level.reshape(1, -1),
            skip.reshape(1, -1),
            jnp.asarray(features, jnp.float32),
            jnp.asarray(forward, jnp.bfloat16),
            jnp.asarray(inverse, jnp.bfloat16),
            weight,
        )

    placed = (
        P("seq", "chan"),
        P("seq", "chan"),
        P("seq", "chan"),
        P(),
        P(),
        P(None, "chan"),
        P("chan"),
        P("chan"),
        P(None, "chan"),
    )
    return jax.shard_map(
        body, mesh=mesh, in_specs=placed, out_specs=P("seq", "chan"), check_vma=False
    )
```

profile of v0, /device:TPU:0, one launch (start us, length us, event | category | flops | bytes accessed | tf_op | source)
XLA Modules:
  0.0 34.4 jit_solution(16880387761107209188)
XLA Ops:
  0.0 0.0 copy-start.9
  0.0 0.0 copy-start.10
  0.0 0.0 copy-start.11
  0.0 0.6 %copy-done.9 = f32[64]{0:T(128)S(1)} copy-done((f32[64]{0:T(128)S(1)}, f32[64]{0:T(128)}, u32[]{:S(2)}) %copy-start.9) | copy-done | bytes 280
  0.7 0.0 copy-done.10
  0.7 0.0 copy-done.11
  0.7 0.0 copy-start
  0.7 1.2 %copy-done = bf16[4096,128]{1,0:T(8,128)(2,1)S(1)} copy-done((bf16[4096,128]{1,0:T(8,128)(2,1)S(1)}, bf16[4096,128]{1,0:T(8,128)(2,1)}, u32[]{:S(2)}) %copy-start) | copy-done | bytes 1048600
  1.9 0.0 copy-start.1
  1.9 1.0 %copy-done.1 = f32[4,256,32]{2,1,0:T(8,128)S(1)} copy-done((f32[4,256,32]{2,1,0:T(8,128)S(1)}, f32[4,256,32]{2,1,0:T(8,128)}, u32[]{:S(2)}) %copy-start.1) | copy-done | bytes 131096
  3.0 0.0 copy-start.2
  3.0 0.9 %copy-done.2 = bf16[256,512]{1,0:T(8,128)(2,1)S(1)} copy-done((bf16[256,512]{1,0:T(8,128)(2,1)S(1)}, bf16[256,512]{1,0:T(8,128)(2,1)}, u32[]{:S(2)}) %copy-start.2) | copy-done | bytes 262168
  3.9 0.0 copy-start.3
  3.9 0.9 %copy-done.3 = bf16[512,256]{1,0:T(8,128)(2,1)S(1)} copy-done((bf16[512,256]{1,0:T(8,128)(2,1)S(1)}, bf16[512,256]{1,0:T(8,128)(2,1)}, u32[]{:S(2)}) %copy-start.3) | copy-done | bytes 262168
  4.9 0.0 copy-start.4
  4.9 0.8 %copy-done.4 = bf16[256,128]{1,0:T(8,128)(2,1)S(1)} copy-done((bf16[256,128]{1,0:T(8,128)(2,1)S(1)}, bf16[256,128]{1,0:T(8,128)(2,1)}, u32[]{:S(2)}) %copy-start.4) | copy-done | bytes 65560
  5.7 0.0 copy-start.5
  5.7 0.8 %copy-done.5 = bf16[256,128]{1,0:T(8,128)(2,1)S(1)} copy-done((bf16[256,128]{1,0:T(8,128)(2,1)S(1)}, bf16[256,128]{1,0:T(8,128)(2,1)}, u32[]{:S(2)}) %copy-start.5) | copy-done | bytes 65560
  6.5 0.0 copy-start.6
  6.5 0.8 %copy-done.6 = bf16[256,128]{1,0:T(8,128)(2,1)S(1)} copy-done((bf16[256,128]{1,0:T(8,128)(2,1)S(1)}, bf16[256,128]{1,0:T(8,128)(2,1)}, u32[]{:S(2)}) %copy-start.6) | copy-done | bytes 65560
  7.4 0.0 copy-start.7
  7.4 0.8 %copy-done.7 = f32[64,128]{1,0:T(8,128)S(1)} copy-done((f32[64,128]{1,0:T(8,128)S(1)}, f32[64,128]{1,0:T(8,128)}, u32[]{:S(2)}) %copy-start.7) | copy-done | bytes 32792
  8.1 0.0 copy-start.8
  8.1 0.7 %copy-done.8 = f32[32,64]{1,0:T(8,128)S(1)} copy-done((f32[32,64]{1,0:T(8,128)S(1)}, f32[32,64]{1,0:T(8,128)}, u32[]{:S(2)}) %copy-start.8) | copy-done | bytes 8216
  8.9 24.9 %shard_map.118 = bf16[256,512]{1,0:T(8,128)(2,1)S(1)} custom-call(bf16[256,128]{1,0:T(8,128)(2,1)S(1)} %copy-done.4, bf16[256,128]{1,0:T(8,128)(2,1)S(1)} %copy-done.5, bf16[256,128]{1,0:T(8,128)(2,1)S(1)} %copy-done.6, f32[32,64]{1,0:T(8,128)S(1)} %copy-done.8, f32[1,64]{1,0:T(1,128)S(1)} %bitcast.3, f32[64,128]{1,0:T(8,128)S(1)} %copy-done.7, ...), custom_call_target="tpu_custom_call" | custom-call | tf_op jit(solution)/shard_map/pallas_call | solution.py:241
  33.7 0.7 %copy.14 = bf16[256,512]{1,0:T(8,128)(2,1)} copy(bf16[256,512]{1,0:T(8,128)(2,1)S(1)} %shard_map.118) | data formatting | bytes 524288
Async XLA Ops:
  0.0 0.7 %copy-start.9 = (f32[64]{0:T(128)S(1)}, f32[64]{0:T(128)}, u32[]{:S(2)}) copy-start(f32[64]{0:T(128)} %param.16) | copy-start | bytes 772
  0.0 0.7 %copy-start.10 = (f32[128]{0:T(128)S(1)}, f32[128]{0:T(128)}, u32[]{:S(2)}) copy-start(f32[128]{0:T(128)} %param.18) | copy-start | bytes 1540
  0.0 0.7 %copy-start.11 = (f32[128]{0:T(128)S(1)}, f32[128]{0:T(128)}, u32[]{:S(2)}) copy-start(f32[128]{0:T(128)} %param.19) | copy-start | bytes 1540
  0.7 1.2 %copy-start = (bf16[4096,128]{1,0:T(8,128)(2,1)S(1)}, bf16[4096,128]{1,0:T(8,128)(2,1)}, u32[]{:S(2)}) copy-start(bf16[4096,128]{1,0:T(8,128)(2,1)} %w_ref.1) | copy-start | bytes 3145732
  1.9 1.0 %copy-start.1 = (f32[4,256,32]{2,1,0:T(8,128)S(1)}, f32[4,256,32]{2,1,0:T(8,128)}, u32[]{:S(2)}) copy-start(f32[4,256,32]{2,1,0:T(8,128)} %constant.6.clone.feat_ref) | copy-start | bytes 393220
  3.0 0.9 %copy-start.2 = (bf16[256,512]{1,0:T(8,128)(2,1)S(1)}, bf16[256,512]{1,0:T(8,128)(2,1)}, u32[]{:S(2)}) copy-start(bf16[256,512]{1,0:T(8,128)(2,1)} %constant.8.clone.inv_ref) | copy-start | bytes 786436
  3.9 0.9 %copy-start.3 = (bf16[512,256]{1,0:T(8,128)(2,1)S(1)}, bf16[512,256]{1,0:T(8,128)(2,1)}, u32[]{:S(2)}) copy-start(bf16[512,256]{1,0:T(8,128)(2,1)} %constant.7.clone.fwd_ref) | copy-start | bytes 786436
  4.9 0.8 %copy-start.4 = (bf16[256,128]{1,0:T(8,128)(2,1)S(1)}, bf16[256,128]{1,0:T(8,128)(2,1)}, u32[]{:S(2)}) copy-start(bf16[256,128]{1,0:T(8,128)(2,1)} %q_ref.1) | copy-start | bytes 196612
  5.7 0.8 %copy-start.5 = (bf16[256,128]{1,0:T(8,128)(2,1)S(1)}, bf16[256,128]{1,0:T(8,128)(2,1)}, u32[]{:S(2)}) copy-start(bf16[256,128]{1,0:T(8,128)(2,1)} %k_ref.1) | copy-start | bytes 196612
  6.5 0.8 %copy-start.6 = (bf16[256,128]{1,0:T(8,128)(2,1)S(1)}, bf16[256,128]{1,0:T(8,128)(2,1)}, u32[]{:S(2)}) copy-start(bf16[256,128]{1,0:T(8,128)(2,1)} %v_ref.1) | copy-start | bytes 196612
  7.4 0.8 %copy-start.7 = (f32[64,128]{1,0:T(8,128)S(1)}, f32[64,128]{1,0:T(8,128)}, u32[]{:S(2)}) copy-start(f32[64,128]{1,0:T(8,128)} %fout_ref.1) | copy-start | bytes 98308
  8.1 0.7 %copy-start.8 = (f32[32,64]{1,0:T(8,128)S(1)}, f32[32,64]{1,0:T(8,128)}, u32[]{:S(2)}) copy-start(f32[32,64]{1,0:T(8,128)} %fin_ref.1) | copy-start | bytes 24580
where the time goes:
time: 35 us; the launch traced here: 34.4 us
  Pallas kernels  24.9 us (71%)
  local copies, waits for them, and re-layouts  9.54 us (27%)
    pallas_call x1, Pallas kernels, body(): pl.pallas_call(functools.partial(kernel, n_seq, n_chan), out_shape=jax.Sh...  24.9 us
    unnamed x25, local copies, waits for them, and re-layouts  9.54 us

commit v1 on v0

--- a/solution.py
+++ b/solution.py
@@ -60,19 +60,31 @@
 def kernel(
     n_seq,
     n_chan,
-    q_ref,
+    k_hbm,
+    v_hbm,
+    q_hbm,
+    feat_hbm,
+    fin_hbm,
+    bias_hbm,
+    fout_hbm,
+    level_hbm,
+    fwd_hbm,
+    skip_hbm,
+    inv_hbm,
+    w_ref,
+    out_ref,
     k_ref,
     v_ref,
+    q_ref,
+    feat_ref,
     fin_ref,
     bias_ref,
     fout_ref,
     level_ref,
+    fwd_ref,
     skip_ref,
-    feat_ref,
-    fwd_ref,
     inv_ref,
-    w_ref,
-    out_ref,
+    load_sem,
     x_buf,
     g_buf,
     w_buf,
@@ -84,6 +96,8 @@
     g_recv,
     w_send,
     w_recv,
+    z_send,
+    z_recv,
     own_sem,
 ):
     rows, cols = q_ref.shape
@@ -91,6 +105,8 @@
     width = w_buf.shape[1]
     me_seq = lax.axis_index("seq")
     me_chan = lax.axis_index("chan")
+    paired = n_chan == 8
+    shared = (6, 7) if paired else ()
 
     barrier = pltpu.get_barrier_semaphore()
     for step in range(1, n_seq):
@@ -102,10 +118,24 @@
             barrier, inc=1, device_id={"chan": flipped(me_chan, mask)}, device_id_type=MESH
         )
 
+    sources = (
+        k_hbm, v_hbm, fin_hbm, feat_hbm, bias_hbm, fout_hbm, level_hbm, fwd_hbm, q_hbm, skip_hbm, inv_hbm
+    )
+    targets = (
+        k_ref, v_ref, fin_ref, feat_ref, bias_ref, fout_ref, level_ref, fwd_ref, q_ref, skip_ref, inv_ref
+    )
+    loads = [
+        pltpu.make_async_copy(source, target, load_sem.at[place])
+        for place, (source, target) in enumerate(zip(sources, targets))
+    ]
+    for load in loads:
+        load.start()
     own_weight = pltpu.make_async_copy(
         w_ref.at[pl.ds(pl.multiple_of(me_chan * width, width), width)], w_buf.at[0], own_sem
     )
     own_weight.start()
+    loads[0].wait()
+    loads[1].wait()
     mixed_in = k_ref[...].astype(jnp.float32) * v_ref[...].astype(jnp.float32)
     x_buf[0] = mixed_in.astype(jnp.bfloat16)
 
@@ -119,24 +149,46 @@
             device_id_type=MESH,
         )
 
+    part = width // n_seq
+
     def w_copy(mask):
         peer = flipped(me_chan, mask)
+        if mask in shared:
+            start = peer * width + me_seq * part
+            source = w_ref.at[pl.ds(pl.multiple_of(start, part), part)]
+            target = w_buf.at[mask, pl.ds(pl.multiple_of(me_seq * part, part), part)]
+        else:
+            source = w_ref.at[pl.ds(pl.multiple_of(peer * width, width), width)]
+            target = w_buf.at[mask]
         return pltpu.make_async_remote_copy(
-            src_ref=w_ref.at[pl.ds(pl.multiple_of(peer * width, width), width)],
-            dst_ref=w_buf.at[mask],
+            src_ref=source,
+            dst_ref=target,
             send_sem=w_send.at[mask],
             recv_sem=w_recv.at[mask],
             device_id={"chan": peer},
             device_id_type=MESH,
         )
 
+    def z_copy(place, step, arrives=False):
+        owner = lax.rem(me_seq + n_seq - step, n_seq) if arrives else me_seq
+        piece = w_buf.at[shared[place], pl.ds(pl.multiple_of(owner * part, part), part)]
+        return pltpu.make_async_remote_copy(
+            src_ref=piece,
+            dst_ref=piece,
+            send_sem=z_send.at[place, step],
+            recv_sem=z_recv.at[place, step],
+            device_id={"seq": lax.rem(me_seq + step, n_seq)},
+            device_id_type=MESH,
+        )
+
     def g_copy(mask):
+        relayed = paired and mask > 1 and mask % 2 == 1
         return pltpu.make_async_remote_copy(
-            src_ref=g_buf.at[0],
+            src_ref=g_buf.at[mask - 1 if relayed else 0],
             dst_ref=g_buf.at[mask],
             send_sem=g_send.at[mask],
             recv_sem=g_recv.at[mask],
-            device_id={"chan": flipped(me_chan, mask)},
+            device_id={"chan": flipped(me_chan, 1 if relayed else mask)},
             device_id_type=MESH,
         )
 
@@ -146,6 +198,8 @@
     for mask in reversed(range(1, n_chan)):
         w_copy(mask).start()
 
+    for load in loads[2:8]:
+        load.wait()
     levels = jnp.maximum(2.0 * level_ref[...] - 1.0, 0.0)
     rate = 0.5 / length * jnp.exp(levels * math.log(length / 16.0))
     fin = fin_ref[...] * (0.5 / math.pi)
@@ -173,6 +227,11 @@
     else:
         squares = lax.fori_loop(0, n_seq, tap_block, squares)
     scale = lax.rsqrt(squares + 1e-05)
+
+    for place, mask in enumerate(shared):
+        w_copy(mask).wait_recv()
+        for step in range(1, n_seq):
+            z_copy(place, step).start()
 
     row_index = lax.broadcasted_iota(jnp.int32, (rows, cols), 0)
     alternate = (1 - 2 * (row_index % 2)).astype(jnp.float32)
@@ -194,6 +253,8 @@
         else:
             pl.when(me_seq >= step)(lambda step=step: add_block(step))
 
+    for load in loads[8:]:
+        load.wait()
     edge = row_index == 0
     y_cos = acc[0] - jnp.where(edge, 0.0, acc[1])
     y_sin = jnp.where(edge, acc[1], acc[2])
@@ -204,26 +265,39 @@
     mixed_in = k_ref[...].astype(jnp.float32) * v_ref[...].astype(jnp.float32)
     gated = q_ref[...].astype(jnp.float32) * (convolved * scale + skip_ref[...] * mixed_in)
     g_buf[0] = gated.astype(jnp.bfloat16)
-    for mask in reversed(range(1, n_chan)):
+    far = range(2, n_chan, 2 if paired else 1)
+    for mask in reversed(far):
         g_copy(mask).start()
-
+    g_copy(1).start()
     own_weight.wait()
     total = None
     for pair in range(0, n_chan, 2):
         for mask in (pair, pair + 1):
-            if mask > 0:
+            if mask == 0:
+                continue
+            if mask in shared:
+                for step in range(1, n_seq):
+                    z_copy(shared.index(mask), step, True).wait_recv()
+            else:
                 w_copy(mask).wait_recv()
+            if not (paired and mask in far):
                 g_copy(mask).wait_recv()
         left = jnp.concatenate([g_buf[pair], g_buf[pair + 1]], axis=1)
         right = jnp.concatenate([w_buf[pair], w_buf[pair + 1]], axis=1)
-        part = lax.dot_general(
+        product = lax.dot_general(
             left, right, (((1,), (1,)), ((), ())), preferred_element_type=jnp.float32
         )
-        total = part if total is None else total + part
+        total = product if total is None else total + product
+        if paired and pair == 0:
+            for mask in far:
+                g_copy(mask).wait_recv()
+                g_copy(mask + 1).start()
     out_ref[...] = total.astype(out_ref.dtype)
 
     for step in range(1, n_seq):
         pl.when(me_seq + step < n_seq)(lambda step=step: x_copy(step).wait_send())
+        for place in range(len(shared)):
+            z_copy(place, step).wait_send()
     for mask in range(1, n_chan):
         w_copy(mask).wait_send()
         g_copy(mask).wait_send()
@@ -237,13 +311,27 @@
         width = weight.shape[0] // n_chan
         forward, inverse = dft_tables(rows)
         features = feature_table(fin.shape[0] // 2, n_seq, rows)
-        vmem = pl.BlockSpec(memory_space=pltpu.VMEM)
+        operands = (
+            key,
+            value,
+            query,
+            jnp.asarray(features, jnp.float32),
+            fin,
+            bias.reshape(1, -1),
+            fout,
+            level.reshape(1, -1),
+            jnp.asarray(forward, jnp.bfloat16),
+            skip.reshape(1, -1),
+            jnp.asarray(inverse, jnp.bfloat16),
+        )
         return pl.pallas_call(
             functools.partial(kernel, n_seq, n_chan),
             out_shape=jax.ShapeDtypeStruct((rows, width), jnp.bfloat16),
-            in_specs=[vmem] * 11 + [pl.BlockSpec(memory_space=pl.ANY)],
-            out_specs=vmem,
-            scratch_shapes=[
+            in_specs=[pl.BlockSpec(memory_space=pltpu.HBM)] * (len(operands) + 1),
+            out_specs=pl.BlockSpec(memory_space=pltpu.VMEM),
+            scratch_shapes=[pltpu.VMEM(item.shape, item.dtype) for item in operands]
+            + [
+                pltpu.SemaphoreType.DMA((len(operands),)),
                 pltpu.VMEM((n_seq, rows, cols), jnp.bfloat16),
                 pltpu.VMEM((n_chan, rows, cols), jnp.bfloat16),
                 pltpu.VMEM((n_chan, width, cols), jnp.bfloat16),
@@ -255,25 +343,14 @@
                 pltpu.SemaphoreType.DMA((n_chan,)),
                 pltpu.SemaphoreType.DMA((n_chan,)),
                 pltpu.SemaphoreType.DMA((n_chan,)),
+                pltpu.SemaphoreType.DMA((2, n_seq)),
+                pltpu.SemaphoreType.DMA((2, n_seq)),
                 pltpu.SemaphoreType.DMA,
             ],
             compiler_params=pltpu.CompilerParams(
-                collective_id=0, has_side_effects=True, vmem_limit_bytes=40 * 1024 * 1024
+                collective_id=0, has_side_effects=True, vmem_limit_bytes=63 * 1024 * 1024
             ),
-        )(
-            query,
-            key,
-            value,
-            fin,
-            bias.reshape(1, -1),
-            fout,
-            level.reshape(1, -1),
-            skip.reshape(1, -1),
-            jnp.asarray(features, jnp.float32),
-            jnp.asarray(forward, jnp.bfloat16),
-            jnp.asarray(inverse, jnp.bfloat16),
-            weight,
-        )
+        )(*operands, weight)
 
     placed = (
         P("seq", "chan"),

time: 35 us -> 22.1 us (0.63)
  the two profiles are of different devices: /device:TPU:0 before, /device:TPU:29 now
where the time goes in v1:
time: 22.1 us; the launch traced here: 22 us
  Pallas kernels  20.3 us (92%)
  local copies, waits for them, and re-layouts  1.67 us (8%)
    pallas_call x1, Pallas kernels, body(): pl.pallas_call(functools.partial(kernel, n_seq, n_chan), out_shape=jax.Sh...  20.3 us
    unnamed x1, local copies, waits for them, and re-layouts  1.67 us

profile of v1, /device:TPU:29, one launch (start us, length us, event | category | flops | bytes accessed | tf_op | source)
XLA Modules:
  0.0 22.0 jit_solution(1630518930237758201)
XLA Ops:
  0.0 20.3 %shard_map.118 = bf16[256,512]{1,0:T(8,128)(2,1)} custom-call(bf16[256,128]{1,0:T(8,128)(2,1)} %k_hbm.1, bf16[256,128]{1,0:T(8,128)(2,1)} %v_hbm.1, bf16[256,128]{1,0:T(8,128)(2,1)} %q_hbm.1, f32[4,256,32]{2,1,0:T(8,128)} %constant.6.clone.feat_hbm, f32[32,64]{1,0:T(8,128)} %fin_hbm.1, f32[1,64]{1,0:T(1,128)} %bitcast.3, f32[64,128]{1,0:T(8,128)} %fout_hbm.1, ...), custom_call_target="tpu_custom_call" | custom-call | tf_op jit(solution)/shard_map/pallas_call | solution.py:327
  20.3 1.7 %copy.14 = bf16[256,512]{1,0:T(8,128)(2,1)} copy(bf16[256,512]{1,0:T(8,128)(2,1)} %shard_map.118) | data formatting | bytes 524288

commit v2 on v1

--- a/solution.py
+++ b/solution.py
@@ -3,6 +3,7 @@
 
 import jax
 import jax.numpy as jnp
+import ml_dtypes
 import numpy as np
 from jax import lax
 from jax.experimental import pallas as pl
@@ -10,7 +11,7 @@
 from jax.sharding import PartitionSpec as P
 
 MESH = pl.DeviceIdType.MESH
-highest = lax.Precision.HIGHEST
+products = ((0, 0), (0, 1), (1, 0), (0, 2), (1, 1), (2, 0))
 
 
 def flipped(index, mask):
@@ -43,8 +44,30 @@
     length = seq_count * rows
     freq = np.arange(1, half_count + 1)
     phases = (np.arange(length)[:, None] * freq[None, :] % length) * (2.0 * math.pi / length)
-    table = np.concatenate([np.sin(phases), np.cos(phases)], axis=1)
-    return table.reshape(seq_count, rows, 2 * half_count)
+    table = np.concatenate([np.sin(phases), np.cos(phases)], axis=1).astype(np.float32)
+    table = table.reshape(seq_count // 2, 2, rows, 2 * half_count)
+    table = np.concatenate([table[:, 0], table[:, 1]], axis=2)
+    terms = []
+    for unused in range(3):
+        terms.append(table.astype(ml_dtypes.bfloat16))
+        table = table - terms[-1].astype(np.float32)
+    return np.concatenate([terms[left] for left, right in products], axis=2)
+
+
+def split(value, count):
+    terms = []
+    for place in range(count):
+        terms.append(value.astype(jnp.bfloat16))
+        if place + 1 < count:
+            value = value - terms[-1].astype(jnp.float32)
+    return terms
+
+
+def twice(block):
+    empty = jnp.zeros_like(block)
+    return jnp.concatenate(
+        [jnp.concatenate([block, empty], axis=1), jnp.concatenate([empty, block], axis=1)], axis=0
+    )
 
 
 def sin_turns(turns):
@@ -195,54 +218,65 @@
     pl.semaphore_wait(barrier, n_seq + n_chan - 2)
     for step in range(1, n_seq):
         pl.when(me_seq + step < n_seq)(lambda step=step: x_copy(step).start())
-    for mask in reversed(range(1, n_chan)):
+    for mask in (6, 7, 4, 2, 5, 3, 1) if paired else reversed(range(1, n_chan)):
         w_copy(mask).start()
 
     for load in loads[2:8]:
         load.wait()
     levels = jnp.maximum(2.0 * level_ref[...] - 1.0, 0.0)
     rate = 0.5 / length * jnp.exp(levels * math.log(length / 16.0))
-    fin = fin_ref[...] * (0.5 / math.pi)
+    row_index = lax.broadcasted_iota(jnp.int32, (rows, cols), 0)
+    alternate = (1 - 2 * (row_index % 2)).astype(jnp.float32)
+    alternate = jnp.concatenate([alternate, alternate], axis=0)
+    decay = jnp.exp(-rate * row_index.astype(jnp.float32))
+    decay = jnp.concatenate([decay, decay], axis=1)
     bias = bias_ref[...] * (0.5 / math.pi)
-    fout = fout_ref[...]
-
-    def tap_block(block, squares):
-        turns = jnp.dot(
-            feat_ref[block], fin, precision=highest, preferred_element_type=jnp.float32
-        )
-        hidden = sin_turns(turns + bias)
-        raw = jnp.dot(hidden, fout, precision=highest, preferred_element_type=jnp.float32)
-        place = lax.broadcasted_iota(jnp.int32, (rows, cols), 0) + block * rows
-        taps = raw * jnp.exp(-rate * place.astype(jnp.float32))
-        spec[block + 1] = jnp.dot(
+    bias = jnp.concatenate([bias, bias], axis=1)
+    first = [twice(term) for term in split(fin_ref[...] * (0.5 / math.pi), 3)]
+    first = jnp.concatenate([first[right] for left, right in products], axis=0)
+    second = [twice(term) for term in split(fout_ref[...], 2)]
+    second = jnp.concatenate([second[0], second[0], second[1]], axis=0)
+
+    def tap_pair(pair, squares):
+        turns = jnp.dot(feat_ref[pair], first, preferred_element_type=jnp.float32)
+        high, low = split(sin_turns(turns + bias), 2)
+        hidden = jnp.concatenate([high, low, high], axis=1)
+        raw = jnp.dot(hidden, second, preferred_element_type=jnp.float32)
+        starts = [rate * -(rows * (2 * pair + side)) for side in (0, 1)]
+        taps = raw * (decay * jnp.exp(jnp.concatenate(starts, axis=1)))
+        both = jnp.dot(
             fwd_ref[...], taps.astype(jnp.bfloat16), preferred_element_type=jnp.float32
         )
+        early, late = both[:, :cols], both[:, cols:]
+        spec[2 * pair] += alternate * early
+        spec[2 * pair + 1] = early + alternate * late
+        if n_seq <= 4:
+            if 2 * pair + 2 < n_seq:
+                spec[2 * pair + 2] = late
+        else:
+            pl.when(2 * pair + 2 < n_seq)(lambda: spec.__setitem__(2 * pair + 2, late))
         return squares + jnp.sum(taps * taps, axis=0, keepdims=True)
 
     spec[0] = jnp.zeros_like(spec[0])
-    squares = jnp.zeros((1, cols), jnp.float32)
+    squares = jnp.zeros((1, 2 * cols), jnp.float32)
     if n_seq <= 4:
-        for block in range(n_seq):
-            squares = tap_block(block, squares)
+        for pair in range(n_seq // 2):
+            squares = tap_pair(pair, squares)
     else:
-        squares = lax.fori_loop(0, n_seq, tap_block, squares)
-    scale = lax.rsqrt(squares + 1e-05)
+        squares = lax.fori_loop(0, n_seq // 2, tap_pair, squares)
+    scale = lax.rsqrt(squares[:, :cols] + squares[:, cols:] + 1e-05)
 
     for place, mask in enumerate(shared):
         w_copy(mask).wait_recv()
         for step in range(1, n_seq):
             z_copy(place, step).start()
-
-    row_index = lax.broadcasted_iota(jnp.int32, (rows, cols), 0)
-    alternate = (1 - 2 * (row_index % 2)).astype(jnp.float32)
 
     def add_block(step):
         if step > 0:
             x_copy(step).wait_recv()
         field = jnp.dot(fwd_ref[...], x_buf[step], preferred_element_type=jnp.float32)
         x_cos, x_sin = field[:rows], field[rows:]
-        h_cos = spec[step, :rows] + alternate * spec[step + 1, :rows]
-        h_sin = spec[step, rows:] + alternate * spec[step + 1, rows:]
+        h_cos, h_sin = spec[step, :rows], spec[step, rows:]
         terms = (x_cos * h_cos, x_sin * h_sin, x_cos * h_sin + x_sin * h_cos)
         for place, term in enumerate(terms):
             acc[place] = term if step == 0 else acc[place] + term
@@ -315,7 +349,7 @@
             key,
             value,
             query,
-            jnp.asarray(features, jnp.float32),
+            jnp.asarray(features),
             fin,
             bias.reshape(1, -1),
             fout,
@@ -326,7 +360,7 @@
         )
         return pl.pallas_call(
             functools.partial(kernel, n_seq, n_chan),
-            out_shape=jax.ShapeDtypeStruct((rows, width), jnp.bfloat16),
+            out_shape=pltpu.VMEM((rows, width), jnp.bfloat16),
             in_specs=[pl.BlockSpec(memory_space=pltpu.HBM)] * (len(operands) + 1),
             out_specs=pl.BlockSpec(memory_space=pltpu.VMEM),
             scratch_shapes=[pltpu.VMEM(item.shape, item.dtype) for item in operands]
@@ -335,7 +369,7 @@
                 pltpu.VMEM((n_seq, rows, cols), jnp.bfloat16),
                 pltpu.VMEM((n_chan, rows, cols), jnp.bfloat16),
                 pltpu.VMEM((n_chan, width, cols), jnp.bfloat16),
-                pltpu.VMEM((n_seq + 1, 2 * rows, cols), jnp.float32),
+                pltpu.VMEM((n_seq, 2 * rows, cols), jnp.float32),
                 pltpu.VMEM((3, rows, cols), jnp.float32),
                 pltpu.SemaphoreType.DMA((n_seq,)),
                 pltpu.SemaphoreType.DMA((n_seq,)),

time: 22.1 us -> 21.5 us (0.973)
  local copies, waits for them, and re-layouts: 1.67 us -> 0.71 us
  Pallas kernels: 20.3 us -> 20.7 us
    unnamed x1, local copies, waits for them, and re-layouts: 1.67 us -> 0.71 us
    pallas_call x1, Pallas kernels: 20.3 us -> 20.7 us  [body(): pl.pallas_call(functools.partial(kernel, n_seq, n_chan), out_shape=pltpu....]
where the time goes in v2:
time: 21.5 us; the launch traced here: 21.4 us
  Pallas kernels  20.7 us (96%)
  local copies, waits for them, and re-layouts  0.71 us (3%)
    pallas_call x1, Pallas kernels, body(): pl.pallas_call(functools.partial(kernel, n_seq, n_chan), out_shape=pltpu....  20.7 us
    unnamed x1, local copies, waits for them, and re-layouts  0.71 us

profile of v2, /device:TPU:29, one launch (start us, length us, event | category | flops | bytes accessed | tf_op | source)
XLA Modules:
  0.0 21.4 jit_solution(17132708836217558073)
XLA Ops:
  0.0 20.7 %shard_map.118 = bf16[256,512]{1,0:T(8,128)(2,1)S(1)} custom-call(bf16[256,128]{1,0:T(8,128)(2,1)} %k_hbm.1, bf16[256,128]{1,0:T(8,128)(2,1)} %v_hbm.1, bf16[256,128]{1,0:T(8,128)(2,1)} %q_hbm.1, bf16[2,256,384]{2,1,0:T(8,128)(2,1)} %constant.6.clone.feat_hbm, f32[32,64]{1,0:T(8,128)} %fin_hbm.1, f32[1,64]{1,0:T(1,128)} %bitcast.3, f32[64,128]{1,0:T(8,128)} %fout_hbm.1, ...), custom_call_target="tpu_custom_call" | custom-call | tf_op jit(solution)/shard_map/pallas_call | solution.py:361
  20.7 0.7 %copy.14 = bf16[256,512]{1,0:T(8,128)(2,1)} copy(bf16[256,512]{1,0:T(8,128)(2,1)S(1)} %shard_map.118) | data formatting | bytes 524288

commit v3 on v2

--- a/solution.py
+++ b/solution.py
@@ -128,7 +128,7 @@
     width = w_buf.shape[1]
     me_seq = lax.axis_index("seq")
     me_chan = lax.axis_index("chan")
-    paired = n_chan == 8
+    paired = n_chan == 8 and n_seq % 2 == 0
     shared = (6, 7) if paired else ()
 
     barrier = pltpu.get_barrier_semaphore()
@@ -172,14 +172,14 @@
             device_id_type=MESH,
         )
 
-    part = width // n_seq
+    part = width // 2
 
     def w_copy(mask):
         peer = flipped(me_chan, mask)
         if mask in shared:
-            start = peer * width + me_seq * part
+            start = peer * width + lax.rem(me_seq, 2) * part
             source = w_ref.at[pl.ds(pl.multiple_of(start, part), part)]
-            target = w_buf.at[mask, pl.ds(pl.multiple_of(me_seq * part, part), part)]
+            target = w_buf.at[mask, pl.ds(pl.multiple_of(lax.rem(me_seq, 2) * part, part), part)]
         else:
             source = w_ref.at[pl.ds(pl.multiple_of(peer * width, width), width)]
             target = w_buf.at[mask]
@@ -192,15 +192,15 @@
             device_id_type=MESH,
         )
 
-    def z_copy(place, step, arrives=False):
-        owner = lax.rem(me_seq + n_seq - step, n_seq) if arrives else me_seq
-        piece = w_buf.at[shared[place], pl.ds(pl.multiple_of(owner * part, part), part)]
+    def z_copy(place, arrives=False):
+        half = lax.rem(me_seq + 1, 2) if arrives else lax.rem(me_seq, 2)
+        piece = w_buf.at[shared[place], pl.ds(pl.multiple_of(half * part, part), part)]
         return pltpu.make_async_remote_copy(
             src_ref=piece,
             dst_ref=piece,
-            send_sem=z_send.at[place, step],
-            recv_sem=z_recv.at[place, step],
-            device_id={"seq": lax.rem(me_seq + step, n_seq)},
+            send_sem=z_send.at[place],
+            recv_sem=z_recv.at[place],
+            device_id={"seq": flipped(me_seq, 1)},
             device_id_type=MESH,
         )
 
@@ -216,7 +216,7 @@
         )
 
     pl.semaphore_wait(barrier, n_seq + n_chan - 2)
-    for step in range(1, n_seq):
+    for step in reversed(range(1, n_seq)):
         pl.when(me_seq + step < n_seq)(lambda step=step: x_copy(step).start())
     for mask in (6, 7, 4, 2, 5, 3, 1) if paired else reversed(range(1, n_chan)):
         w_copy(mask).start()
@@ -266,11 +266,6 @@
         squares = lax.fori_loop(0, n_seq // 2, tap_pair, squares)
     scale = lax.rsqrt(squares[:, :cols] + squares[:, cols:] + 1e-05)
 
-    for place, mask in enumerate(shared):
-        w_copy(mask).wait_recv()
-        for step in range(1, n_seq):
-            z_copy(place, step).start()
-
     def add_block(step):
         if step > 0:
             x_copy(step).wait_recv()
@@ -303,6 +298,9 @@
     for mask in reversed(far):
         g_copy(mask).start()
     g_copy(1).start()
+    for place, mask in enumerate(shared):
+        w_copy(mask).wait_recv()
+        z_copy(place).start()
     own_weight.wait()
     total = None
     for pair in range(0, n_chan, 2):
@@ -310,8 +308,7 @@
             if mask == 0:
                 continue
             if mask in shared:
-                for step in range(1, n_seq):
-                    z_copy(shared.index(mask), step, True).wait_recv()
+                z_copy(shared.index(mask), True).wait_recv()
             else:
                 w_copy(mask).wait_recv()
             if not (paired and mask in far):
@@ -330,8 +327,8 @@
 
     for step in range(1, n_seq):
         pl.when(me_seq + step < n_seq)(lambda step=step: x_copy(step).wait_send())
-        for place in range(len(shared)):
-            z_copy(place, step).wait_send()
+    for place in range(len(shared)):
+        z_copy(place).wait_send()
     for mask in range(1, n_chan):
         w_copy(mask).wait_send()
         g_copy(mask).wait_send()
@@ -377,8 +374,8 @@
                 pltpu.SemaphoreType.DMA((n_chan,)),
                 pltpu.SemaphoreType.DMA((n_chan,)),
                 pltpu.SemaphoreType.DMA((n_chan,)),
-                pltpu.SemaphoreType.DMA((2, n_seq)),
-                pltpu.SemaphoreType.DMA((2, n_seq)),
+                pltpu.SemaphoreType.DMA((2,)),
+                pltpu.SemaphoreType.DMA((2,)),
                 pltpu.SemaphoreType.DMA,
             ],
             compiler_params=pltpu.CompilerParams(

time: 21.5 us -> 21.3 us (level)
  the two profiles are of different devices: /device:TPU:29 before, /device:TPU:1 now
where the time goes in v3:
time: 21.3 us; the launch traced here: 21.1 us
  Pallas kernels  20.4 us (96%)
  local copies, waits for them, and re-layouts  0.71 us (3%)
    pallas_call x1, Pallas kernels, body(): pl.pallas_call(functools.partial(kernel, n_seq, n_chan), out_shape=pltpu....  20.4 us
    unnamed x1, local copies, waits for them, and re-layouts  0.71 us

profile of v3, /device:TPU:1, one launch (start us, length us, event | category | flops | bytes accessed | tf_op | source)
XLA Modules:
  0.0 21.1 jit_solution(4852212242253370101)
XLA Ops:
  0.0 20.4 %shard_map.118 = bf16[256,512]{1,0:T(8,128)(2,1)S(1)} custom-call(bf16[256,128]{1,0:T(8,128)(2,1)} %k_hbm.1, bf16[256,128]{1,0:T(8,128)(2,1)} %v_hbm.1, bf16[256,128]{1,0:T(8,128)(2,1)} %q_hbm.1, bf16[2,256,384]{2,1,0:T(8,128)(2,1)} %constant.6.clone.feat_hbm, f32[32,64]{1,0:T(8,128)} %fin_hbm.1, f32[1,64]{1,0:T(1,128)} %bitcast.3, f32[64,128]{1,0:T(8,128)} %fout_hbm.1, ...), custom_call_target="tpu_custom_call" | custom-call | tf_op jit(solution)/shard_map/pallas_call | solution.py:358
  20.4 0.7 %copy.14 = bf16[256,512]{1,0:T(8,128)(2,1)} copy(bf16[256,512]{1,0:T(8,128)(2,1)S(1)} %shard_map.118) | data formatting | bytes 524288

commit v4 on v3

--- a/solution.py
+++ b/solution.py
@@ -129,7 +129,7 @@
     me_seq = lax.axis_index("seq")
     me_chan = lax.axis_index("chan")
     paired = n_chan == 8 and n_seq % 2 == 0
-    shared = (6, 7) if paired else ()
+    fetched = {6: 2, 7: 2, 4: 3, 2: 3, 5: 3, 3: 3} if paired else {}
 
     barrier = pltpu.get_barrier_semaphore()
     for step in range(1, n_seq):
@@ -172,34 +172,34 @@
             device_id_type=MESH,
         )
 
-    part = width // 2
+    piece = width // 4
+    odd = lax.rem(me_seq, 2)
+
+    def block_rows(start, count):
+        return pl.ds(pl.multiple_of(start, piece), count)
 
     def w_copy(mask):
         peer = flipped(me_chan, mask)
-        if mask in shared:
-            start = peer * width + lax.rem(me_seq, 2) * part
-            source = w_ref.at[pl.ds(pl.multiple_of(start, part), part)]
-            target = w_buf.at[mask, pl.ds(pl.multiple_of(lax.rem(me_seq, 2) * part, part), part)]
-        else:
-            source = w_ref.at[pl.ds(pl.multiple_of(peer * width, width), width)]
-            target = w_buf.at[mask]
+        count = fetched.get(mask, 4) * piece
+        start = odd * (width - count)
         return pltpu.make_async_remote_copy(
-            src_ref=source,
-            dst_ref=target,
+            src_ref=w_ref.at[block_rows(peer * width + start, count)],
+            dst_ref=w_buf.at[mask, block_rows(start, count)],
             send_sem=w_send.at[mask],
             recv_sem=w_recv.at[mask],
             device_id={"chan": peer},
             device_id_type=MESH,
         )
 
-    def z_copy(place, arrives=False):
-        half = lax.rem(me_seq + 1, 2) if arrives else lax.rem(me_seq, 2)
-        piece = w_buf.at[shared[place], pl.ds(pl.multiple_of(half * part, part), part)]
+    def z_copy(mask, arrives=False):
+        count = (4 - fetched[mask]) * piece
+        side = 1 - odd if arrives else odd
+        part = w_buf.at[mask, block_rows(side * (width - count), count)]
         return pltpu.make_async_remote_copy(
-            src_ref=piece,
-            dst_ref=piece,
-            send_sem=z_send.at[place],
-            recv_sem=z_recv.at[place],
+            src_ref=part,
+            dst_ref=part,
+            send_sem=z_send.at[mask],
+            recv_sem=z_recv.at[mask],
             device_id={"seq": flipped(me_seq, 1)},
             device_id_type=MESH,
         )
@@ -298,17 +298,19 @@
     for mask in reversed(far):
         g_copy(mask).start()
     g_copy(1).start()
-    for place, mask in enumerate(shared):
+    for step in range(1, n_seq):
+        pl.when(me_seq + step < n_seq)(lambda step=step: x_copy(step).wait_send())
+    for mask in fetched:
         w_copy(mask).wait_recv()
-        z_copy(place).start()
+        z_copy(mask).start()
     own_weight.wait()
     total = None
     for pair in range(0, n_chan, 2):
         for mask in (pair, pair + 1):
             if mask == 0:
                 continue
-            if mask in shared:
-                z_copy(shared.index(mask), True).wait_recv()
+            if mask in fetched:
+                z_copy(mask, True).wait_recv()
             else:
                 w_copy(mask).wait_recv()
             if not (paired and mask in far):
@@ -325,10 +327,8 @@
                 g_copy(mask + 1).start()
     out_ref[...] = total.astype(out_ref.dtype)
 
-    for step in range(1, n_seq):
-        pl.when(me_seq + step < n_seq)(lambda step=step: x_copy(step).wait_send())
-    for place in range(len(shared)):
-        z_copy(place).wait_send()
+    for mask in fetched:
+        z_copy(mask).wait_send()
     for mask in range(1, n_chan):
         w_copy(mask).wait_send()
         g_copy(mask).wait_send()
@@ -374,8 +374,8 @@
                 pltpu.SemaphoreType.DMA((n_chan,)),
                 pltpu.SemaphoreType.DMA((n_chan,)),
                 pltpu.SemaphoreType.DMA((n_chan,)),
-                pltpu.SemaphoreType.DMA((2,)),
-                pltpu.SemaphoreType.DMA((2,)),
+                pltpu.SemaphoreType.DMA((n_chan,)),
+                pltpu.SemaphoreType.DMA((n_chan,)),
                 pltpu.SemaphoreType.DMA,
             ],
             compiler_params=pltpu.CompilerParams(

time: 21.3 us -> 20 us (0.939)
  the two profiles are of different devices: /device:TPU:1 before, /device:TPU:0 now
where the time goes in v4:
time: 20 us; the launch traced here: 19.8 us
  Pallas kernels  19.1 us (96%)
  local copies, waits for them, and re-layouts  0.71 us (4%)
    pallas_call x1, Pallas kernels, body(): pl.pallas_call(functools.partial(kernel, n_seq, n_chan), out_shape=pltpu....  19.1 us
    unnamed x1, local copies, waits for them, and re-layouts  0.71 us

profile of v4, /device:TPU:0, one launch (start us, length us, event | category | flops | bytes accessed | tf_op | source)
XLA Modules:
  0.0 19.8 jit_solution(4744500270980635637)
XLA Ops:
  0.0 19.1 %shard_map.118 = bf16[256,512]{1,0:T(8,128)(2,1)S(1)} custom-call(bf16[256,128]{1,0:T(8,128)(2,1)} %k_hbm.1, bf16[256,128]{1,0:T(8,128)(2,1)} %v_hbm.1, bf16[256,128]{1,0:T(8,128)(2,1)} %q_hbm.1, bf16[2,256,384]{2,1,0:T(8,128)(2,1)} %constant.6.clone.feat_hbm, f32[32,64]{1,0:T(8,128)} %fin_hbm.1, f32[1,64]{1,0:T(1,128)} %bitcast.3, f32[64,128]{1,0:T(8,128)} %fout_hbm.1, ...), custom_call_target="tpu_custom_call" | custom-call | tf_op jit(solution)/shard_map/pallas_call | solution.py:358
  19.1 0.7 %copy.14 = bf16[256,512]{1,0:T(8,128)(2,1)} copy(bf16[256,512]{1,0:T(8,128)(2,1)S(1)} %shard_map.118) | data formatting | bytes 524288

commit v5 on v4

--- a/solution.py
+++ b/solution.py
@@ -68,6 +68,33 @@
     return jnp.concatenate(
         [jnp.concatenate([block, empty], axis=1), jnp.concatenate([empty, block], axis=1)], axis=0
     )
+
+
+def regroup(blocks):
+    count, lanes = len(blocks), blocks[0].shape[1]
+    width = lanes // count
+    group = lax.broadcasted_iota(jnp.int32, blocks[0].shape, 1) // width
+    results = []
+    for target in range(count):
+        result = None
+        for place, block in enumerate(blocks):
+            shift = (place - target) % count * width
+            moved = pltpu.roll(block, shift, 1) if shift else block
+            result = moved if result is None else jnp.where(group == place, moved, result)
+        results.append(result)
+    return results
+
+
+def spread(value, index, count):
+    width = value.shape[1] // count
+    group = lax.broadcasted_iota(jnp.int32, value.shape, 1) // width
+    chosen = value
+    for place in range(1, count):
+        chosen = jnp.where(index == place, pltpu.roll(value, (count - place) * width, 1), chosen)
+    result = chosen
+    for place in range(1, count):
+        result = jnp.where(group == place, pltpu.roll(chosen, place * width, 1), result)
+    return result
 
 
 def sin_turns(turns):
@@ -122,6 +149,9 @@
     z_send,
     z_recv,
     own_sem,
+    e_buf,
+    y_send,
+    y_recv,
 ):
     rows, cols = q_ref.shape
     length = rows * n_seq
@@ -160,7 +190,38 @@
     loads[0].wait()
     loads[1].wait()
     mixed_in = k_ref[...].astype(jnp.float32) * v_ref[...].astype(jnp.float32)
-    x_buf[0] = mixed_in.astype(jnp.bfloat16)
+    swap = n_seq == 4
+    slab = rows // n_seq
+
+    def store_pieces(value, place):
+        pieces = regroup([value[slab * i : slab * (i + 1)] for i in range(n_seq)])
+        for i, piece in enumerate(pieces):
+            e_buf[place, i] = piece.astype(jnp.bfloat16)
+
+            @pl.when(me_seq == i)
+            def own_piece(i=i):
+                e_buf[place + 1, i] = e_buf[place, i]
+
+
+    def load_pieces(place):
+        pieces = regroup([e_buf[place, i].astype(jnp.float32) for i in range(n_seq)])
+        return jnp.concatenate(pieces, axis=0)
+
+    def swap_copy(place, step):
+        peer = lax.rem(me_seq + step, n_seq)
+        return pltpu.make_async_remote_copy(
+            src_ref=e_buf.at[place, peer],
+            dst_ref=e_buf.at[place + 1, me_seq],
+            send_sem=(x_send if place == 0 else y_send).at[step],
+            recv_sem=(x_recv if place == 0 else y_recv).at[step],
+            device_id={"seq": peer},
+            device_id_type=MESH,
+        )
+
+    if swap:
+        store_pieces(mixed_in, 0)
+    else:
+        x_buf[0] = mixed_in.astype(jnp.bfloat16)
 
     def x_copy(step):
         return pltpu.make_async_remote_copy(
@@ -217,88 +278,176 @@
 
     pl.semaphore_wait(barrier, n_seq + n_chan - 2)
     for step in reversed(range(1, n_seq)):
+        if swap:
+            swap_copy(0, step).start()
+            continue
         pl.when(me_seq + step < n_seq)(lambda step=step: x_copy(step).start())
     for mask in (6, 7, 4, 2, 5, 3, 1) if paired else reversed(range(1, n_chan)):
         w_copy(mask).start()
 
     for load in loads[2:8]:
         load.wait()
-    levels = jnp.maximum(2.0 * level_ref[...] - 1.0, 0.0)
-    rate = 0.5 / length * jnp.exp(levels * math.log(length / 16.0))
-    row_index = lax.broadcasted_iota(jnp.int32, (rows, cols), 0)
-    alternate = (1 - 2 * (row_index % 2)).astype(jnp.float32)
-    alternate = jnp.concatenate([alternate, alternate], axis=0)
-    decay = jnp.exp(-rate * row_index.astype(jnp.float32))
-    decay = jnp.concatenate([decay, decay], axis=1)
-    bias = bias_ref[...] * (0.5 / math.pi)
-    bias = jnp.concatenate([bias, bias], axis=1)
-    first = [twice(term) for term in split(fin_ref[...] * (0.5 / math.pi), 3)]
-    first = jnp.concatenate([first[right] for left, right in products], axis=0)
-    second = [twice(term) for term in split(fout_ref[...], 2)]
-    second = jnp.concatenate([second[0], second[0], second[1]], axis=0)
-
-    def tap_pair(pair, squares):
-        turns = jnp.dot(feat_ref[pair], first, preferred_element_type=jnp.float32)
-        high, low = split(sin_turns(turns + bias), 2)
-        hidden = jnp.concatenate([high, low, high], axis=1)
+    def gathered():
+        levels = jnp.maximum(2.0 * level_ref[...] - 1.0, 0.0)
+        rate = 0.5 / length * jnp.exp(levels * math.log(length / 16.0))
+        row_index = lax.broadcasted_iota(jnp.int32, (rows, cols), 0)
+        alternate = (1 - 2 * (row_index % 2)).astype(jnp.float32)
+        alternate = jnp.concatenate([alternate, alternate], axis=0)
+        decay = jnp.exp(-rate * row_index.astype(jnp.float32))
+        decay = jnp.concatenate([decay, decay], axis=1)
+        bias = bias_ref[...] * (0.5 / math.pi)
+        bias = jnp.concatenate([bias, bias], axis=1)
+        first = [twice(term) for term in split(fin_ref[...] * (0.5 / math.pi), 3)]
+        first = jnp.concatenate([first[right] for left, right in products], axis=0)
+        second = [twice(term) for term in split(fout_ref[...], 2)]
+        second = jnp.concatenate([second[0], second[0], second[1]], axis=0)
+
+        def tap_pair(pair, squares):
+            turns = jnp.dot(feat_ref[pair], first, preferred_element_type=jnp.float32)
+            high, low = split(sin_turns(turns + bias), 2)
+            hidden = jnp.concatenate([high, low, high], axis=1)
+            raw = jnp.dot(hidden, second, preferred_element_type=jnp.float32)
+            starts = [rate * -(rows * (2 * pair + side)) for side in (0, 1)]
+            taps = raw * (decay * jnp.exp(jnp.concatenate(starts, axis=1)))
+            both = jnp.dot(
+                fwd_ref[...], taps.astype(jnp.bfloat16), preferred_element_type=jnp.float32
+            )
+            early, late = both[:, :cols], both[:, cols:]
+            spec[2 * pair] += alternate * early
+            spec[2 * pair + 1] = early + alternate * late
+            if n_seq <= 4:
+                if 2 * pair + 2 < n_seq:
+                    spec[2 * pair + 2] = late
+            else:
+                pl.when(2 * pair + 2 < n_seq)(lambda: spec.__setitem__(2 * pair + 2, late))
+            return squares + jnp.sum(taps * taps, axis=0, keepdims=True)
+
+        spec[0] = jnp.zeros_like(spec[0])
+        squares = jnp.zeros((1, 2 * cols), jnp.float32)
+        if n_seq <= 4:
+            for pair in range(n_seq // 2):
+                squares = tap_pair(pair, squares)
+        else:
+            squares = lax.fori_loop(0, n_seq // 2, tap_pair, squares)
+        scale = lax.rsqrt(squares[:, :cols] + squares[:, cols:] + 1e-05)
+
+        def add_block(step):
+            if step > 0:
+                x_copy(step).wait_recv()
+            field = jnp.dot(fwd_ref[...], x_buf[step], preferred_element_type=jnp.float32)
+            x_cos, x_sin = field[:rows], field[rows:]
+            h_cos, h_sin = spec[step, :rows], spec[step, rows:]
+            terms = (x_cos * h_cos, x_sin * h_sin, x_cos * h_sin + x_sin * h_cos)
+            for place, term in enumerate(terms):
+                acc[place] = term if step == 0 else acc[place] + term
+
+        for step in range(n_seq):
+            if step == 0:
+                add_block(step)
+            else:
+                pl.when(me_seq >= step)(lambda step=step: add_block(step))
+
+        for load in loads[8:]:
+            load.wait()
+        edge = row_index == 0
+        y_cos = acc[0] - jnp.where(edge, 0.0, acc[1])
+        y_sin = jnp.where(edge, acc[1], acc[2])
+        field = jnp.concatenate([y_cos, y_sin], axis=0) * (0.5 / rows)
+        return scale * jnp.dot(
+            inv_ref[...], field.astype(jnp.bfloat16), preferred_element_type=jnp.float32
+        )
+
+    def swapped():
+        width = cols // n_seq
+        lane_group = lax.broadcasted_iota(jnp.int32, (rows, cols), 1) // width
+        row_index = lax.broadcasted_iota(jnp.int32, (rows, cols), 0)
+        alternate = (1 - 2 * (row_index % 2)).astype(jnp.float32)
+        alternate = jnp.concatenate([alternate, alternate], axis=0)
+        tall_group = jnp.concatenate([lane_group, lane_group], axis=0)
+        level = jnp.broadcast_to(level_ref[...], (8, cols))
+        levels = jnp.maximum(2.0 * spread(level, me_seq, n_seq)[:1] - 1.0, 0.0)
+        rate = 0.5 / length * jnp.exp(levels * math.log(length / 16.0))
+        bias = bias_ref[...] * (0.5 / math.pi)
+        bias = jnp.concatenate([bias, bias], axis=1)
+        first = [twice(term) for term in split(fin_ref[...] * (0.5 / math.pi), 3)]
+        first = jnp.concatenate([first[right] for left, right in products], axis=0)
+        fout = spread(fout_ref[...], me_seq, n_seq)
+        fout_group = lax.broadcasted_iota(jnp.int32, fout.shape, 1) // width
+        fout = jnp.concatenate(
+            [jnp.where(fout_group == i, fout, 0.0) for i in range(n_seq)], axis=0
+        )
+        second = split(fout, 2)
+        second = jnp.concatenate([second[0], second[0], second[1]], axis=0)
+        highs, lows = [], []
+        for pair in range(n_seq // 2):
+            turns = jnp.dot(feat_ref[pair], first, preferred_element_type=jnp.float32)
+            high, low = split(sin_turns(turns + bias), 2)
+            highs.append(high)
+            lows.append(low)
+        hidden = jnp.concatenate(highs + lows + highs, axis=1)
         raw = jnp.dot(hidden, second, preferred_element_type=jnp.float32)
-        starts = [rate * -(rows * (2 * pair + side)) for side in (0, 1)]
-        taps = raw * (decay * jnp.exp(jnp.concatenate(starts, axis=1)))
-        both = jnp.dot(
+        taps = raw * jnp.exp(-rate * (row_index + rows * lane_group).astype(jnp.float32))
+        squares = jnp.sum(taps * taps, axis=0, keepdims=True)
+        squares = jnp.broadcast_to(squares, (8, cols))
+        total = squares
+        for place in range(1, n_seq):
+            total = total + pltpu.roll(squares, place * width, 1)
+        scale = lax.rsqrt(total[:1] + 1e-05)
+        blocks = jnp.dot(
             fwd_ref[...], taps.astype(jnp.bfloat16), preferred_element_type=jnp.float32
         )
-        early, late = both[:, :cols], both[:, cols:]
-        spec[2 * pair] += alternate * early
-        spec[2 * pair + 1] = early + alternate * late
-        if n_seq <= 4:
-            if 2 * pair + 2 < n_seq:
-                spec[2 * pair + 2] = late
-        else:
-            pl.when(2 * pair + 2 < n_seq)(lambda: spec.__setitem__(2 * pair + 2, late))
-        return squares + jnp.sum(taps * taps, axis=0, keepdims=True)
-
-    spec[0] = jnp.zeros_like(spec[0])
-    squares = jnp.zeros((1, 2 * cols), jnp.float32)
-    if n_seq <= 4:
-        for pair in range(n_seq // 2):
-            squares = tap_pair(pair, squares)
-    else:
-        squares = lax.fori_loop(0, n_seq // 2, tap_pair, squares)
-    scale = lax.rsqrt(squares[:, :cols] + squares[:, cols:] + 1e-05)
-
-    def add_block(step):
-        if step > 0:
-            x_copy(step).wait_recv()
-        field = jnp.dot(fwd_ref[...], x_buf[step], preferred_element_type=jnp.float32)
-        x_cos, x_sin = field[:rows], field[rows:]
-        h_cos, h_sin = spec[step, :rows], spec[step, rows:]
-        terms = (x_cos * h_cos, x_sin * h_sin, x_cos * h_sin + x_sin * h_cos)
-        for place, term in enumerate(terms):
-            acc[place] = term if step == 0 else acc[place] + term
-
-    for step in range(n_seq):
-        if step == 0:
-            add_block(step)
-        else:
-            pl.when(me_seq >= step)(lambda step=step: add_block(step))
-
-    for load in loads[8:]:
-        load.wait()
-    edge = row_index == 0
-    y_cos = acc[0] - jnp.where(edge, 0.0, acc[1])
-    y_sin = jnp.where(edge, acc[1], acc[2])
-    field = jnp.concatenate([y_cos, y_sin], axis=0) * (0.5 / rows)
-    convolved = jnp.dot(
-        inv_ref[...], field.astype(jnp.bfloat16), preferred_element_type=jnp.float32
-    )
+        before = jnp.where(tall_group > 0, pltpu.roll(blocks, width, 1), 0.0)
+        window = before + alternate * blocks
+        for place in range(n_seq):
+            chosen = window
+            for target in range(n_seq):
+                if target != place:
+                    shift = (target - place) % n_seq * width
+                    chosen = jnp.where(
+                        tall_group == target, pltpu.roll(window, shift, 1), chosen
+                    )
+            spec[place] = jnp.where(tall_group >= place, chosen, 0.0)
+        for step in range(1, n_seq):
+            swap_copy(0, step).wait_recv()
+        tokens = load_pieces(1).astype(jnp.bfloat16)
+        field = jnp.dot(fwd_ref[...], tokens, preferred_element_type=jnp.float32)
+        sums = None
+        for place in range(n_seq):
+            moved = pltpu.roll(field, place * width, 1) if place else field
+            x_cos, x_sin = moved[:rows], moved[rows:]
+            h_cos, h_sin = spec[place, :rows], spec[place, rows:]
+            terms = (x_cos * h_cos, x_sin * h_sin, x_cos * h_sin + x_sin * h_cos)
+            sums = terms if sums is None else [a + b for a, b in zip(sums, terms)]
+        edge = row_index == 0
+        y_cos = sums[0] - jnp.where(edge, 0.0, sums[1])
+        y_sin = jnp.where(edge, sums[1], sums[2])
+        result = jnp.concatenate([y_cos, y_sin], axis=0) * (0.5 / rows)
+        loads[10].wait()
+        result = scale * jnp.dot(
+            inv_ref[...], result.astype(jnp.bfloat16), preferred_element_type=jnp.float32
+        )
+        store_pieces(result, 2)
+        for step in reversed(range(1, n_seq)):
+            swap_copy(2, step).start()
+        for load in loads[8:10]:
+            load.wait()
+        for step in range(1, n_seq):
+            swap_copy(2, step).wait_recv()
+        return load_pieces(3)
+
+    convolved = swapped() if swap else gathered()
     mixed_in = k_ref[...].astype(jnp.float32) * v_ref[...].astype(jnp.float32)
-    gated = q_ref[...].astype(jnp.float32) * (convolved * scale + skip_ref[...] * mixed_in)
+    gated = q_ref[...].astype(jnp.float32) * (convolved + skip_ref[...] * mixed_in)
     g_buf[0] = gated.astype(jnp.bfloat16)
     far = range(2, n_chan, 2 if paired else 1)
     for mask in reversed(far):
         g_copy(mask).start()
     g_copy(1).start()
     for step in range(1, n_seq):
+        if swap:
+            swap_copy(0, step).wait_send()
+            swap_copy(2, step).wait_send()
+            continue
         pl.when(me_seq + step < n_seq)(lambda step=step: x_copy(step).wait_send())
     for mask in fetched:
         w_copy(mask).wait_recv()
@@ -377,6 +526,9 @@
                 pltpu.SemaphoreType.DMA((n_chan,)),
                 pltpu.SemaphoreType.DMA((n_chan,)),
                 pltpu.SemaphoreType.DMA,
+                pltpu.VMEM((4, n_seq, rows // n_seq, cols), jnp.bfloat16),
+                pltpu.SemaphoreType.DMA((n_seq,)),
+                pltpu.SemaphoreType.DMA((n_seq,)),
             ],
             compiler_params=pltpu.CompilerParams(
                 collective_id=0, has_side_effects=True, vmem_limit_bytes=63 * 1024 * 1024

time: 20 us -> 22 us (1.10)
  Pallas kernels: 19.1 us -> 21.1 us
    pallas_call x1, Pallas kernels: 19.1 us -> 21.1 us  [body(): pl.pallas_call(functools.partial(kernel, n_seq, n_chan), out_shape=pltpu....]
where the time goes in v5:
time: 22 us; the launch traced here: 21.9 us
  Pallas kernels  21.1 us (96%)
  local copies, waits for them, and re-layouts  0.71 us (3%)
    pallas_call x1, Pallas kernels, body(): pl.pallas_call(functools.partial(kernel, n_seq, n_chan), out_shape=pltpu....  21.1 us
    unnamed x1, local copies, waits for them, and re-layouts  0.71 us

profile of v5, /device:TPU:0, one launch (start us, length us, event | category | flops | bytes accessed | tf_op | source)
XLA Modules:
  0.0 21.9 jit_solution(6258003770340414099)
XLA Ops:
  0.0 21.1 %shard_map.118 = bf16[256,512]{1,0:T(8,128)(2,1)S(1)} custom-call(bf16[256,128]{1,0:T(8,128)(2,1)} %k_hbm.1, bf16[256,128]{1,0:T(8,128)(2,1)} %v_hbm.1, bf16[256,128]{1,0:T(8,128)(2,1)} %q_hbm.1, bf16[2,256,384]{2,1,0:T(8,128)(2,1)} %constant.6.clone.feat_hbm, f32[32,64]{1,0:T(8,128)} %fin_hbm.1, f32[1,64]{1,0:T(1,128)} %bitcast.3, f32[64,128]{1,0:T(8,128)} %fout_hbm.1, ...), custom_call_target="tpu_custom_call" | custom-call | tf_op jit(solution)/shard_map/pallas_call | solution.py:507
  21.2 0.7 %copy.14 = bf16[256,512]{1,0:T(8,128)(2,1)} copy(bf16[256,512]{1,0:T(8,128)(2,1)S(1)} %shard_map.118) | data formatting | bytes 524288

commit v6 on v4

--- a/solution.py
+++ b/solution.py
@@ -178,15 +178,20 @@
     def block_rows(start, count):
         return pl.ds(pl.multiple_of(start, piece), count)
 
-    def w_copy(mask):
+    def w_copy(mask, first=False):
         peer = flipped(me_chan, mask)
-        count = fetched.get(mask, 4) * piece
-        start = odd * (width - count)
+        count = (4 - fetched.get(mask, 4)) * piece
+        start = count
+        if first:
+            start = odd * (width - count)
+        else:
+            count = width - 2 * count
+        place = mask + n_chan if first else mask
         return pltpu.make_async_remote_copy(
             src_ref=w_ref.at[block_rows(peer * width + start, count)],
             dst_ref=w_buf.at[mask, block_rows(start, count)],
-            send_sem=w_send.at[mask],
-            recv_sem=w_recv.at[mask],
+            send_sem=w_send.at[place],
+            recv_sem=w_recv.at[place],
             device_id={"chan": peer},
             device_id_type=MESH,
         )
@@ -218,8 +223,15 @@
     pl.semaphore_wait(barrier, n_seq + n_chan - 2)
     for step in reversed(range(1, n_seq)):
         pl.when(me_seq + step < n_seq)(lambda step=step: x_copy(step).start())
-    for mask in (6, 7, 4, 2, 5, 3, 1) if paired else reversed(range(1, n_chan)):
+    for mask in fetched:
+        w_copy(mask, True).start()
+    kept = [mask for mask in (4, 2, 5, 3, 1) if paired] or list(reversed(range(1, n_chan)))
+    for mask in kept:
         w_copy(mask).start()
+
+    def forward(mask):
+        w_copy(mask, True).wait_recv()
+        z_copy(mask).start()
 
     for load in loads[2:8]:
         load.wait()
@@ -279,6 +291,9 @@
     for step in range(n_seq):
         if step == 0:
             add_block(step)
+            for mask in fetched:
+                if mask not in kept:
+                    pl.when(odd == 1)(lambda mask=mask: forward(mask))
         else:
             pl.when(me_seq >= step)(lambda step=step: add_block(step))
 
@@ -301,8 +316,10 @@
     for step in range(1, n_seq):
         pl.when(me_seq + step < n_seq)(lambda step=step: x_copy(step).wait_send())
     for mask in fetched:
-        w_copy(mask).wait_recv()
-        z_copy(mask).start()
+        if mask in kept:
+            forward(mask)
+        else:
+            pl.when(odd == 0)(lambda mask=mask: forward(mask))
     own_weight.wait()
     total = None
     for pair in range(0, n_chan, 2):
@@ -311,7 +328,7 @@
                 continue
             if mask in fetched:
                 z_copy(mask, True).wait_recv()
-            else:
+            if mask in kept:
                 w_copy(mask).wait_recv()
             if not (paired and mask in far):
                 g_copy(mask).wait_recv()
@@ -329,8 +346,10 @@
 
     for mask in fetched:
         z_copy(mask).wait_send()
+        w_copy(mask, True).wait_send()
     for mask in range(1, n_chan):
-        w_copy(mask).wait_send()
+        if mask in kept:
+            w_copy(mask).wait_send()
         g_copy(mask).wait_send()
 
 
@@ -372,8 +391,8 @@
                 pltpu.SemaphoreType.DMA((n_seq,)),
                 pltpu.SemaphoreType.DMA((n_chan,)),
                 pltpu.SemaphoreType.DMA((n_chan,)),
-                pltpu.SemaphoreType.DMA((n_chan,)),
-                pltpu.SemaphoreType.DMA((n_chan,)),
+                pltpu.SemaphoreType.DMA((2 * n_chan,)),
+                pltpu.SemaphoreType.DMA((2 * n_chan,)),
                 pltpu.SemaphoreType.DMA((n_chan,)),
                 pltpu.SemaphoreType.DMA((n_chan,)),
                 pltpu.SemaphoreType.DMA,

time: 20 us -> 20.1 us (level)
  no operation moved by 1% of the time
where the time goes in v6:
time: 20.1 us; the launch traced here: 19.8 us
  Pallas kernels  19.1 us (95%)
  local copies, waits for them, and re-layouts  0.71 us (4%)
    pallas_call x1, Pallas kernels, body(): pl.pallas_call(functools.partial(kernel, n_seq, n_chan), out_shape=pltpu....  19.1 us
    unnamed x1, local copies, waits for them, and re-layouts  0.71 us

profile of v6, /device:TPU:0, one launch (start us, length us, event | category | flops | bytes accessed | tf_op | source)
XLA Modules:
  0.0 19.8 jit_solution(7725322249632742135)
XLA Ops:
  0.0 19.1 %shard_map.118 = bf16[256,512]{1,0:T(8,128)(2,1)S(1)} custom-call(bf16[256,128]{1,0:T(8,128)(2,1)} %k_hbm.1, bf16[256,128]{1,0:T(8,128)(2,1)} %v_hbm.1, bf16[256,128]{1,0:T(8,128)(2,1)} %q_hbm.1, bf16[2,256,384]{2,1,0:T(8,128)(2,1)} %constant.6.clone.feat_hbm, f32[32,64]{1,0:T(8,128)} %fin_hbm.1, f32[1,64]{1,0:T(1,128)} %bitcast.3, f32[64,128]{1,0:T(8,128)} %fout_hbm.1, ...), custom_call_target="tpu_custom_call" | custom-call | tf_op jit(solution)/shard_map/pallas_call | solution.py:377
  19.1 0.7 %copy.14 = bf16[256,512]{1,0:T(8,128)(2,1)} copy(bf16[256,512]{1,0:T(8,128)(2,1)S(1)} %shard_map.118) | data formatting | bytes 524288

commit v7 on v6

--- a/solution.py
+++ b/solution.py
@@ -338,8 +338,8 @@
             left, right, (((1,), (1,)), ((), ())), preferred_element_type=jnp.float32
         )
         total = product if total is None else total + product
-        if paired and pair == 0:
-            for mask in far:
+        if paired and pair < 4:
+            for mask in (2, 4) if pair == 0 else (6,):
                 g_copy(mask).wait_recv()
                 g_copy(mask + 1).start()
     out_ref[...] = total.astype(out_ref.dtype)

time: 20.1 us -> 21.2 us (1.055)
  Pallas kernels: 19.1 us -> 20.3 us
    pallas_call x1, Pallas kernels: 19.1 us -> 20.3 us  [body(): pl.pallas_call(functools.partial(kernel, n_seq, n_chan), out_shape=pltpu....]
where the time goes in v7:
time: 21.2 us; the launch traced here: 21 us
  Pallas kernels  20.3 us (96%)
  local copies, waits for them, and re-layouts  0.71 us (3%)
    pallas_call x1, Pallas kernels, body(): pl.pallas_call(functools.partial(kernel, n_seq, n_chan), out_shape=pltpu....  20.3 us
    unnamed x1, local copies, waits for them, and re-layouts  0.71 us

profile of v7, /device:TPU:0, one launch (start us, length us, event | category | flops | bytes accessed | tf_op | source)
XLA Modules:
  0.0 21.0 jit_solution(5022948162088300000)
XLA Ops:
  0.0 20.3 %shard_map.118 = bf16[256,512]{1,0:T(8,128)(2,1)S(1)} custom-call(bf16[256,128]{1,0:T(8,128)(2,1)} %k_hbm.1, bf16[256,128]{1,0:T(8,128)(2,1)} %v_hbm.1, bf16[256,128]{1,0:T(8,128)(2,1)} %q_hbm.1, bf16[2,256,384]{2,1,0:T(8,128)(2,1)} %constant.6.clone.feat_hbm, f32[32,64]{1,0:T(8,128)} %fin_hbm.1, f32[1,64]{1,0:T(1,128)} %bitcast.3, f32[64,128]{1,0:T(8,128)} %fout_hbm.1, ...), custom_call_target="tpu_custom_call" | custom-call | tf_op jit(solution)/shard_map/pallas_call | solution.py:377
  20.3 0.7 %copy.14 = bf16[256,512]{1,0:T(8,128)(2,1)} copy(bf16[256,512]{1,0:T(8,128)(2,1)S(1)} %shard_map.118) | data formatting | bytes 524288

commit v8 on v6

--- a/solution.py
+++ b/solution.py
@@ -292,8 +292,7 @@
         if step == 0:
             add_block(step)
             for mask in fetched:
-                if mask not in kept:
-                    pl.when(odd == 1)(lambda mask=mask: forward(mask))
+                forward(mask)
         else:
             pl.when(me_seq >= step)(lambda step=step: add_block(step))
 
@@ -315,11 +314,6 @@
     g_copy(1).start()
     for step in range(1, n_seq):
         pl.when(me_seq + step < n_seq)(lambda step=step: x_copy(step).wait_send())
-    for mask in fetched:
-        if mask in kept:
-            forward(mask)
-        else:
-            pl.when(odd == 0)(lambda mask=mask: forward(mask))
     own_weight.wait()
     total = None
     for pair in range(0, n_chan, 2):

time: 20.1 us -> 20.7 us (1.030)
  Pallas kernels: 19.1 us -> 19.9 us
    pallas_call x1, Pallas kernels: 19.1 us -> 19.9 us  [body(): pl.pallas_call(functools.partial(kernel, n_seq, n_chan), out_shape=pltpu....]
where the time goes in v8:
time: 20.7 us; the launch traced here: 20.6 us
  Pallas kernels  19.9 us (96%)
  local copies, waits for them, and re-layouts  0.71 us (3%)
    pallas_call x1, Pallas kernels, body(): pl.pallas_call(functools.partial(kernel, n_seq, n_chan), out_shape=pltpu....  19.9 us
    unnamed x1, local copies, waits for them, and re-layouts  0.71 us

profile of v8, /device:TPU:0, one launch (start us, length us, event | category | flops | bytes accessed | tf_op | source)
XLA Modules:
  0.0 20.6 jit_solution(2559874958060801349)
XLA Ops:
  0.0 19.9 %shard_map.118 = bf16[256,512]{1,0:T(8,128)(2,1)S(1)} custom-call(bf16[256,128]{1,0:T(8,128)(2,1)} %k_hbm.1, bf16[256,128]{1,0:T(8,128)(2,1)} %v_hbm.1, bf16[256,128]{1,0:T(8,128)(2,1)} %q_hbm.1, bf16[2,256,384]{2,1,0:T(8,128)(2,1)} %constant.6.clone.feat_hbm, f32[32,64]{1,0:T(8,128)} %fin_hbm.1, f32[1,64]{1,0:T(1,128)} %bitcast.3, f32[64,128]{1,0:T(8,128)} %fout_hbm.1, ...), custom_call_target="tpu_custom_call" | custom-call | tf_op jit(solution)/shard_map/pallas_call | solution.py:371
  19.9 0.7 %copy.14 = bf16[256,512]{1,0:T(8,128)(2,1)} copy(bf16[256,512]{1,0:T(8,128)(2,1)S(1)} %shard_map.118) | data formatting | bytes 524288

commit v9 on v7

--- a/solution.py
+++ b/solution.py
@@ -320,6 +320,10 @@
             forward(mask)
         else:
             pl.when(odd == 0)(lambda mask=mask: forward(mask))
+    if paired:
+        for mask in far:
+            g_copy(mask).wait_recv()
+            g_copy(mask + 1).start()
     own_weight.wait()
     total = None
     for pair in range(0, n_chan, 2):
@@ -338,10 +342,6 @@
             left, right, (((1,), (1,)), ((), ())), preferred_element_type=jnp.float32
         )
         total = product if total is None else total + product
-        if paired and pair < 4:
-            for mask in (2, 4) if pair == 0 else (6,):
-                g_copy(mask).wait_recv()
-                g_copy(mask + 1).start()
     out_ref[...] = total.astype(out_ref.dtype)
 
     for mask in fetched:

time: 21.2 us -> 20.1 us (0.948)
  Pallas kernels: 20.3 us -> 19.1 us
    pallas_call x1, Pallas kernels: 20.3 us -> 19.1 us  [body(): pl.pallas_call(functools.partial(kernel, n_seq, n_chan), out_shape=pltpu....]
where the time goes in v9:
time: 20.1 us; the launch traced here: 19.8 us
  Pallas kernels  19.1 us (95%)
  local copies, waits for them, and re-layouts  0.71 us (4%)
    pallas_call x1, Pallas kernels, body(): pl.pallas_call(functools.partial(kernel, n_seq, n_chan), out_shape=pltpu....  19.1 us
    unnamed x1, local copies, waits for them, and re-layouts  0.71 us

profile of v9, /device:TPU:0, one launch (start us, length us, event | category | flops | bytes accessed | tf_op | source)
XLA Modules:
  0.0 19.8 jit_solution(15642696316878511913)
XLA Ops:
  0.0 19.1 %shard_map.118 = bf16[256,512]{1,0:T(8,128)(2,1)S(1)} custom-call(bf16[256,128]{1,0:T(8,128)(2,1)} %k_hbm.1, bf16[256,128]{1,0:T(8,128)(2,1)} %v_hbm.1, bf16[256,128]{1,0:T(8,128)(2,1)} %q_hbm.1, bf16[2,256,384]{2,1,0:T(8,128)(2,1)} %constant.6.clone.feat_hbm, f32[32,64]{1,0:T(8,128)} %fin_hbm.1, f32[1,64]{1,0:T(1,128)} %bitcast.3, f32[64,128]{1,0:T(8,128)} %fout_hbm.1, ...), custom_call_target="tpu_custom_call" | custom-call | tf_op jit(solution)/shard_map/pallas_call | solution.py:377
  19.1 0.7 %copy.14 = bf16[256,512]{1,0:T(8,128)(2,1)} copy(bf16[256,512]{1,0:T(8,128)(2,1)S(1)} %shard_map.118) | data formatting | bytes 524288
